TPU v7x, 32 devices: a whole 2x2x4 slice. The times are simulated.
32 devices in a mesh: groups: 2 (over x), rows: 16 (over z, y, core).
Axes of the slice: x: 2, y: 2, z: 4, core: 2. Of those that a mesh axis runs over, the one named last changes fastest.
Arguments:
- latents: bfloat16 [2, 64, 256, 128], P('groups', 'rows'), parts along dimension 0, may hold values from -60 to 60
- gain_one: float32 [128], replicated, may hold values from 0.25 to 1.75
- shift_one: float32 [128], replicated, may hold values from -3 to 3
- weight_one: bfloat16 [3, 3, 3, 128, 128], replicated, may hold values from -0.109375 to 0.109375
- bias_one: float32 [128], replicated, may hold values from -3 to 3
- gain_two: float32 [128], replicated, may hold values from 0.25 to 1.75
- shift_two: float32 [128], replicated, may hold values from -3 to 3
- weight_two: bfloat16 [3, 3, 3, 128, 128], replicated, may hold values from -0.109375 to 0.109375
- bias_two: float32 [128], replicated, may hold values from -3 to 3
Outputs:
- decoded: bfloat16 [2, 64, 256, 128], P('groups', 'rows'), parts along dimension 0
There are 2 independent parts, one for each index of `groups`. A program takes and returns all parts, laid end to end along the dimension named above; an argument that names none is the same for every part. Nothing has to cross between parts.
All inputs are finite; a program needn't handle non-finite values.
Results may differ from a plain program's by a relative error of at most 0.004.
Values may be sent and summed in bfloat16 or wider, within the bound.
A program may use at most 64 MiB of HBM per device.

v0:
```python
import jax
import jax.numpy as jnp
from jax import lax
from jax.sharding import PartitionSpec as P

GROUPS = 32


def padded_2(block, sides, width):
    for axis, dim in sides:
        count = lax.axis_size(axis)
        forward = [(i, i + 1) for i in range(count - 1)]
        backward = [(target, source) for source, target in forward]
        low = lax.ppermute(
            lax.slice_in_dim(block, block.shape[dim] - width, None, axis=dim), axis, forward
        )
        high = lax.ppermute(lax.slice_in_dim(block, 0, width, axis=dim), axis, backward)
        block = jnp.concatenate([low, block, high], axis=dim)
    return block


def group_stats(values):
    channels = values.shape[3]
    per_group = channels // GROUPS
    count = values.shape[0] * values.shape[1] * values.shape[2] * per_group * lax.axis_size("rows")
    chan_sum = jnp.sum(values, axis=(0, 1, 2))
    chan_square = jnp.sum(values * values, axis=(0, 1, 2))
    totals = lax.psum(
        (chan_sum.reshape(GROUPS, per_group).sum(1), chan_square.reshape(GROUPS, per_group).sum(1)),
        "rows",
    )
    mean = totals[0] / count
    var = totals[1] / count - mean * mean
    inverse = 1.0 / jnp.sqrt(var + 1e-06)
    return (jnp.repeat(mean, per_group), jnp.repeat(inverse, per_group))


def normalize(values, mean_chan, inverse_chan, gain, shift):
    normed = (values - mean_chan) * inverse_chan * gain + shift
    return jax.nn.silu(normed).astype(jnp.bfloat16)


def edge_fix(padded, own, depth):
    index = lax.axis_index("rows")
    last_index = lax.axis_size("rows") - 1
    upper = jnp.where(index == 0, jnp.repeat(own[:, :1], depth, axis=1), padded[:, :depth])
    lower = jnp.where(
        index == last_index, jnp.repeat(own[:, -1:], depth, axis=1), padded[:, -depth:]
    )
    return jnp.concatenate([upper, padded[:, depth:-depth], lower], axis=1)


def row_rims(acts):
    padded = padded_2(acts, (("rows", 1),), 1)
    return edge_fix(padded, acts, 1)


def causal_conv(banded, weight, bias):
    frame_count = banded.shape[0]
    width = banded.shape[2]
    out_rows = banded.shape[1] - 2
    channels = weight.shape[4]
    timed = jnp.concatenate([banded, banded, banded], axis=0)
    widened = jnp.concatenate([timed[:, :, :1], timed, timed[:, :, -1:]], axis=2)
    stacked = jnp.concatenate(
        [widened[:, :, 0:width], widened[:, :, 1 : width + 1], widened[:, :, 2 : width + 2]], axis=3
    )
    total = jnp.zeros((frame_count, out_rows, width, channels), jnp.float32)
    for tap_time in range(3):
        for tap_row in range(3):
            window = stacked[tap_time : tap_time + frame_count, tap_row : tap_row + out_rows]
            kernel = weight[tap_time, tap_row].reshape(3 * weight.shape[3], channels)
            total = total + jnp.dot(window, kernel, preferred_element_type=jnp.float32)
    return total + bias


def body(
    latents, gain_one, shift_one, weight_one, bias_one, gain_two, shift_two, weight_two, bias_two
):
    own = latents.astype(jnp.float32)
    mean_one, inverse_one = group_stats(own)
    act_one = normalize(own, mean_one, inverse_one, gain_one, shift_one)
    hidden = causal_conv(row_rims(act_one), weight_one, bias_one).astype(jnp.bfloat16)
    hidden_float = hidden.astype(jnp.float32)
    mean_two, inverse_two = group_stats(hidden_float)
    act_two = normalize(hidden_float, mean_two, inverse_two, gain_two, shift_two)
    banded_two = row_rims(act_two)
    branch = causal_conv(banded_two, weight_two, bias_two)
    return (own + branch).astype(jnp.bfloat16)


def solution(mesh):
    return jax.shard_map(
        body,
        mesh=mesh,
        in_specs=(P("groups", "rows", None, None), P(), P(), P(), P(), P(), P(), P(), P()),
        out_specs=P("groups", "rows", None, None),
        check_vma=False,
    )
```

profile of v0, /device:TPU:1, one launch (start us, length us, event | category | flops | bytes accessed | tf_op | source)
XLA Modules:
  0.0 90.8 jit_solution(7943135905014250381)
XLA Ops:
  0.0 1.1 %convert_reduce_fusion = (f32[128]{0:T(128)S(1)}, f32[128]{0:T(128)S(1)}) fusion(bf16[1,4,256,128]{3,2,1,0:T(8,128)(2,1)} %param.9), kind=kLoop, calls=%fused_computation.33 | loop fusion | flops 524032 | bytes 263168 | tf_op jit(solution)/shard_map/reduce_sum | solution.py:26
  1.1 0.1 reshape.153
  1.2 0.1 reshape.154
  1.3 0.1 reduce_sum.73
  1.4 0.1 reduce_sum.75
  1.5 30.6 %all-reduce.1 = (f32[32]{0:T(128)S(1)}, f32[32]{0:T(128)S(1)}) all-reduce(f32[32]{0:T(128)S(1)} %reduce_sum.75, f32[32]{0:T(128)S(1)} %reduce_sum.73), channel_id=1, replica_groups=mesh['groups'=2,'rows'=16] {'rows'}, use_global_device_ids=true, to_apply=%region_5.0 | all-reduce | flops 64 | bytes 512 | tf_op jit(solution)/shard_map/psum | solution.py:28
  32.1 0.1 broadcast_in_dim.9
  32.2 0.1 mul.61
  32.4 0.1 sub.27
  32.5 1.2 %fusion.21 = bf16[1,4,256,128]{3,2,1,0:T(8,128)(2,1)S(1)} fusion(bf16[1,4,256,128]{3,2,1,0:T(8,128)(2,1)} %param.9, f32[128]{0:T(128)} %param.11, f32[128]{0:T(128)} %param.10, f32[128]{0:T(128)S(1)} %mul.61, f32[128]{0:T(128)S(1)} %sub.27), kind=kLoop, calls=%fused_computation.62 | loop fusion | flops 1310720 | bytes 526336 | tf_op jit(solution)/shard_map/convert_element_type | solution.py:40
  33.7 3.0 %collective-permute-start = (bf16[1,1,256,128]{3,2,1,0:T(8,128)(2,1)S(1)}, bf16[1,1,256,128]{3,2,1,0:T(8,128)(2,1)S(1)}, u32[]{:S(2)}, u32[]{:S(2)}) collective-permute-start(bf16[1,1,256,128]{3,2,1,0:T(8,128)(2,1)S(1)} %get-tuple-element.41), channel_id=1, source_target_pairs={{0,1},{1,2},{2,3},{3,4},{4,5},{5,6},{6,7},{7,8},{8,9},{9,10},{10,1... | collective-permute-start | bytes 196616 | tf_op jit(solution)/shard_map/ppermute | solution.py:14
  36.7 4.6 %collective-permute-start.1 = (bf16[1,1,256,128]{3,2,1,0:T(8,128)(2,1)S(1)}, bf16[1,1,256,128]{3,2,1,0:T(8,128)(2,1)S(1)}, u32[]{:S(2)}, u32[]{:S(2)}) collective-permute-start(bf16[1,1,256,128]{3,2,1,0:T(8,128)(2,1)S(1)} %get-tuple-element.42), channel_id=1, source_target_pairs={{1,0},{2,1},{3,2},{4,3},{5,4},{6,5},{7,6},{8,7},{9,8},{10,9},{11,1... | collective-permute-start | bytes 196616 | tf_op jit(solution)/shard_map/ppermute | solution.py:17
  41.3 1.3 %fusion.26 = (bf16[1,1,3,128,128]{4,3,2,1,0:T(8,128)(2,1)S(1)}, bf16[1,1,3,128,128]{4,3,2,1,0:T(8,128)(2,1)S(1)}, bf16[1,1,3,128,128]{4,3,2,1,0:T(8,128)(2,1)S(1...) fusion(bf16[3,3,3,128,128]{4,3,2,1,0:T(8,128)(2,1)} %param.12), kind=kLoop, calls=%fused_computation.83 | loop fusion | bytes 1769472 | tf_op jit(solution)/shard_map/slice | solution.py:72
  42.8 0.2 concatenate.47
  43.0 1.2 %fusion.2 = bf16[3,6,256,384]{3,2,1,0:T(8,128)(2,1)S(1)} fusion(bf16[3,6,1,128]{3,2,1,0:T(2,128)(2,1)S(1)} %concatenate.49, bf16[3,6,256,128]{3,2,1,0:T(8,128)(2,1)S(1)} %concatenate.47, bf16[3,6,1,128]{3,2,1,0:T(2,128)(2,1)S(1)} %concatenate.46), kind=kLoop, calls=%fused_computation.5 | loop fusion | flops 17694720 | bytes 4727808 | tf_op jit(solution)/shard_map/concatenate | solution.py:65
  44.3 0.4 fusion.12
  44.7 0.4 convolution_add_fusion.15
  45.0 0.4 convolution_add_fusion.14
  45.4 0.4 convolution_add_fusion.13
  45.8 0.4 convolution_add_fusion.12
  46.2 0.4 convolution_add_fusion.11
  46.6 0.4 convolution_add_fusion.10
  47.0 0.4 convolution_add_fusion.9
  47.3 0.4 fusion.24
  47.8 0.1 reshape.164
  47.9 0.1 reduce_sum.77
  48.0 0.1 reshape.165
  48.1 0.1 reduce_sum.79
  48.2 28.7 %all-reduce = (f32[32]{0:T(128)S(1)}, f32[32]{0:T(128)S(1)}) all-reduce(f32[32]{0:T(128)S(1)} %reduce_sum.79, f32[32]{0:T(128)S(1)} %reduce_sum.77), channel_id=1, replica_groups=mesh['groups'=2,'rows'=16] {'rows'}, use_global_device_ids=true, to_apply=%region_11.12 | all-reduce | flops 64 | bytes 512 | tf_op jit(solution)/shard_map/psum | solution.py:28
  77.0 0.1 broadcast_in_dim.21
  77.0 0.1 mul.69
  77.1 0.1 broadcast_in_dim.20
  77.2 0.1 sub.31
  77.3 0.2 fusion.23
  77.6 1.9 %collective-permute-start.2 = (bf16[1,1,256,128]{3,2,1,0:T(8,128)(2,1)S(1)}, bf16[1,1,256,128]{3,2,1,0:T(8,128)(2,1)S(1)}, u32[]{:S(2)}, u32[]{:S(2)}) collective-permute-start(bf16[1,1,256,128]{3,2,1,0:T(8,128)(2,1)S(1)} %get-tuple-element.37), channel_id=1, source_target_pairs={{0,1},{1,2},{2,3},{3,4},{4,5},{5,6},{6,7},{7,8},{8,9},{9,10},{10,1... | collective-permute-start | bytes 196616 | tf_op jit(solution)/shard_map/ppermute | solution.py:14
  79.5 2.6 %collective-permute-start.3 = (bf16[1,1,256,128]{3,2,1,0:T(8,128)(2,1)S(1)}, bf16[1,1,256,128]{3,2,1,0:T(8,128)(2,1)S(1)}, u32[]{:S(2)}, u32[]{:S(2)}) collective-permute-start(bf16[1,1,256,128]{3,2,1,0:T(8,128)(2,1)S(1)} %get-tuple-element.38), channel_id=1, source_target_pairs={{1,0},{2,1},{3,2},{4,3},{5,4},{6,5},{7,6},{8,7},{9,8},{10,9},{11,1... | collective-permute-start | bytes 196616 | tf_op jit(solution)/shard_map/ppermute | solution.py:17
  82.2 2.9 %collective-permute-done.3 = bf16[1,1,256,128]{3,2,1,0:T(8,128)(2,1)S(1)} collective-permute-done((bf16[1,1,256,128]{3,2,1,0:T(8,128)(2,1)S(1)}, bf16[1,1,256,128]{3,2,1,0:T(8,128)(2,1)S(1)}, u32[]{:S(2)}, u32[]{:S(2)}) %collective-permute-start.3) | collective-permute-done | bytes 65568 | tf_op jit(solution)/shard_map/ppermute | solution.py:17
  85.2 0.2 concatenate.55
  85.5 1.2 %fusion = bf16[3,6,256,384]{3,2,1,0:T(8,128)(2,1)S(1)} fusion(bf16[3,6,1,128]{3,2,1,0:T(2,128)(2,1)S(1)} %concatenate.57, bf16[3,6,256,128]{3,2,1,0:T(8,128)(2,1)S(1)} %concatenate.55, bf16[3,6,1,128]{3,2,1,0:T(2,128)(2,1)S(1)} %concatenate.54), kind=kLoop, calls=%fused_computation.1 | loop fusion | flops 17694720 | bytes 4727808 | tf_op jit(solution)/shard_map/concatenate | solution.py:65
  86.7 0.4 fusion.11
  87.1 0.4 convolution_add_fusion.7
  87.4 0.4 convolution_add_fusion.6
  87.8 0.4 convolution_add_fusion.5
  88.2 0.4 convolution_add_fusion.4
  88.6 0.4 convolution_add_fusion.3
  89.0 0.4 convolution_add_fusion.2
  89.3 0.4 convolution_add_fusion.1
  89.7 1.1 %fusion.10 = bf16[1,4,256,128]{3,2,1,0:T(8,128)(2,1)} fusion(f32[4,256,128]{2,1,0:T(8,128)S(1)} %convolution_add_fusion.1, bf16[384,128,1]{1,0,2:T(8,128)(2,1)S(1)} %bitcast.151, bf16[1,4,256,128]{3,2,1,0:T(8,128)(2,1)S(1)} %copy-done, bf16[3,6,256,384]{3,2,1,0:T(8,128)(2,1)S(1)} %fusion, f32[128]{0:T(128)S(1)} %copy-done.4), kind=kOutput, calls=%fused_computation.30 | convolution fusion | flops 101318656 | bytes 1933824 | tf_op jit(solution)/shard_map/dot_general | solution.py:73
  (34 shorter events, 0.4 us)
Async XLA Ops:
  33.7 8.9 %collective-permute-start = (bf16[1,1,256,128]{3,2,1,0:T(8,128)(2,1)S(1)}, bf16[1,1,256,128]{3,2,1,0:T(8,128)(2,1)S(1)}, u32[]{:S(2)}, u32[]{:S(2)}) collective-permute-start(bf16[1,1,256,128]{3,2,1,0:T(8,128)(2,1)S(1)} %get-tuple-element.41), channel_id=1, source_target_pairs={{0,1},{1,2},{2,3},{3,4},{4,5},{5,6},{6,7},{7,8},{8,9},{9,10},{10,1... | collective-permute-start | bytes 196616 | tf_op jit(solution)/shard_map/ppermute | solution.py:14
  36.7 6.0 %collective-permute-start.1 = (bf16[1,1,256,128]{3,2,1,0:T(8,128)(2,1)S(1)}, bf16[1,1,256,128]{3,2,1,0:T(8,128)(2,1)S(1)}, u32[]{:S(2)}, u32[]{:S(2)}) collective-permute-start(bf16[1,1,256,128]{3,2,1,0:T(8,128)(2,1)S(1)} %get-tuple-element.42), channel_id=1, source_target_pairs={{1,0},{2,1},{3,2},{4,3},{5,4},{6,5},{7,6},{8,7},{9,8},{10,9},{11,1... | collective-permute-start | bytes 196616 | tf_op jit(solution)/shard_map/ppermute | solution.py:17
  45.8 1.5 %copy-start.5 = (f32[128]{0:T(128)S(1)}, f32[128]{0:T(128)}, u32[]{:S(2)}) copy-start(f32[128]{0:T(128)} %param.13) | copy-start | bytes 1540
  46.2 31.1 %copy-start.2 = (f32[128]{0:T(128)S(1)}, f32[128]{0:T(128)}, u32[]{:S(2)}) copy-start(f32[128]{0:T(128)} %param.15) | copy-start | bytes 1540
  46.2 31.1 %copy-start.3 = (f32[128]{0:T(128)S(1)}, f32[128]{0:T(128)}, u32[]{:S(2)}) copy-start(f32[128]{0:T(128)} %param.14) | copy-start | bytes 1540
  46.6 35.5 %copy-start.1 = (bf16[3,3,3,128,128]{4,3,2,1,0:T(8,128)(2,1)S(1)}, bf16[3,3,3,128,128]{4,3,2,1,0:T(8,128)(2,1)}, u32[]{:S(2)}) copy-start(bf16[3,3,3,128,128]{4,3,2,1,0:T(8,128)(2,1)} %param.16) | copy-start | bytes 2654212
  77.6 4.6 %collective-permute-start.2 = (bf16[1,1,256,128]{3,2,1,0:T(8,128)(2,1)S(1)}, bf16[1,1,256,128]{3,2,1,0:T(8,128)(2,1)S(1)}, u32[]{:S(2)}, u32[]{:S(2)}) collective-permute-start(bf16[1,1,256,128]{3,2,1,0:T(8,128)(2,1)S(1)} %get-tuple-element.37), channel_id=1, source_target_pairs={{0,1},{1,2},{2,3},{3,4},{4,5},{5,6},{6,7},{7,8},{8,9},{9,10},{10,1... | collective-permute-start | bytes 196616 | tf_op jit(solution)/shard_map/ppermute | solution.py:14
  79.5 5.6 %collective-permute-start.3 = (bf16[1,1,256,128]{3,2,1,0:T(8,128)(2,1)S(1)}, bf16[1,1,256,128]{3,2,1,0:T(8,128)(2,1)S(1)}, u32[]{:S(2)}, u32[]{:S(2)}) collective-permute-start(bf16[1,1,256,128]{3,2,1,0:T(8,128)(2,1)S(1)} %get-tuple-element.38), channel_id=1, source_target_pairs={{1,0},{2,1},{3,2},{4,3},{5,4},{6,5},{7,6},{8,7},{9,8},{10,9},{11,1... | collective-permute-start | bytes 196616 | tf_op jit(solution)/shard_map/ppermute | solution.py:17
  88.2 1.5 %copy-start = (bf16[1,4,256,128]{3,2,1,0:T(8,128)(2,1)S(1)}, bf16[1,4,256,128]{3,2,1,0:T(8,128)(2,1)}, u32[]{:S(2)}) copy-start(bf16[1,4,256,128]{3,2,1,0:T(8,128)(2,1)} %param.9) | copy-start | bytes 786436
  88.2 1.5 %copy-start.4 = (f32[128]{0:T(128)S(1)}, f32[128]{0:T(128)}, u32[]{:S(2)}) copy-start(f32[128]{0:T(128)} %param.17) | copy-start | bytes 1540
where the time goes:
time: 91.1 us; the launch traced here: 90.8 us
  blocking collectives  59.3 us (65%)
  starting transfers between devices  12.1 us (13%)
  matrix products  7.35 us (8%)
  other arithmetic  5.53 us (6%)
  local copies, waits for them, and re-layouts  3.08 us (3%)
  waiting for transfers between devices  2.88 us (3%)
    psum x2, blocking collectives, group_stats(): lax.psum((chan_sum.reshape(GROUPS, per_group).sum(1), chan_square.reshape...  59.3 us
    dot_general x18, matrix products, causal_conv(): total = total + jnp.dot(window, kernel, preferred_element_type=jnp.float32)  7.35 us
    ppermute x2, starting transfers between devices, padded_2(): lax.ppermute(lax.slice_in_dim(block, 0, width, axis=dim), axis, backward)  7.24 us
    ppermute x2, starting transfers between devices, padded_2(): lax.ppermute(lax.slice_in_dim(block, block.shape[dim] - width, None, axis...  4.9 us
    ppermute x2, waiting for transfers between devices, padded_2(): lax.ppermute(lax.slice_in_dim(block, 0, width, axis=dim), axis, backward)  2.87 us
    concatenate x2, other arithmetic, causal_conv(): jnp.concatenate([widened[:, :, 0:width], widened[:, :, 1:width + 1], wide...  2.46 us
  transfers between devices with their start and end apart: 4, of which 1 were waited for; matrix products, arithmetic and copies ran while one was open for 2% of the time, Pallas kernels for 0%

commit v1 on v0

v1 whole, which is shorter than its diff:
```python
import functools

import jax
import jax.numpy as jnp
from jax import lax
from jax.experimental import pallas as pl
from jax.experimental.pallas import tpu as pltpu
from jax.sharding import PartitionSpec as P

GROUPS = 32
MESH = pl.DeviceIdType.MESH
F32 = jnp.float32
BF16 = jnp.bfloat16


def partial_sums(rows):
    sums, squares = [], []
    for row in rows:
        tiles = row.reshape(row.shape[0] // 8, 8, row.shape[1])
        sums.append(jnp.sum(tiles, axis=0))
        squares.append(jnp.sum(tiles * tiles, axis=0))
    total = functools.reduce(jnp.add, sums)
    square = functools.reduce(jnp.add, squares)
    return jnp.concatenate(
        [jnp.sum(total, axis=0, keepdims=True), jnp.sum(square, axis=0, keepdims=True)], axis=0
    )


def group_total(sums, per_group):
    lane = lax.broadcasted_iota(jnp.int32, sums.shape, 1)
    lanes = sums.shape[1]
    step = 1
    while step < per_group:
        up = pltpu.roll(sums, lanes - step, 1)
        down = pltpu.roll(sums, step, 1)
        sums = sums + jnp.where((lane // step) % 2 == 0, up, down)
        step *= 2
    return sums


def scale_offset(slots, gain, shift, count, per_group):
    totals = group_total(jnp.sum(slots, axis=0), per_group)
    mean = totals[0:1] / count
    var = totals[1:2] / count - mean * mean
    scale = gain / jnp.sqrt(var + 1e-06)
    return scale, shift - mean * scale


def silu(values):
    return values / (1.0 + jnp.exp(-values))


def kernel(
    n,
    count,
    per_group,
    x_hbm, g1_hbm, s1_hbm, w1_hbm, b1_hbm, g2_hbm, s2_hbm, w2_hbm, b2_hbm,
    out_ref,
    x, w1, w2, wp1, wp2, vec, act, stack, hid, own_stat, in_stat,
    load_sem, stat_send, stat_recv, rim_send, rim_recv,
):
    me = lax.axis_index("rows")
    rows = x_hbm.shape[1]
    width = x_hbm.shape[2]
    chan = x_hbm.shape[3]
    band = 3 * chan
    vec_hbm = (g1_hbm, s1_hbm, b1_hbm, g2_hbm, s2_hbm, b2_hbm)

    loads = [pltpu.make_async_copy(x_hbm.at[0], x.at[pl.ds(2, rows)], load_sem.at[0])]
    loads.append(pltpu.make_async_copy(w1_hbm, w1, load_sem.at[1]))
    loads.append(pltpu.make_async_copy(w2_hbm, w2, load_sem.at[2]))
    for i, ref in enumerate(vec_hbm):
        loads.append(pltpu.make_async_copy(ref, vec.at[i], load_sem.at[3 + i]))
    for copy in loads:
        copy.start()

    barrier = pltpu.get_barrier_semaphore()

    def greet(k, carry):
        pl.semaphore_signal(
            barrier, inc=1, device_id={"rows": lax.rem(me + k, n)}, device_id_type=MESH
        )
        return carry

    lax.fori_loop(1, n, greet, 0)

    loads[0].wait()
    own_stat[0] = partial_sums([x[2 + r].astype(F32) for r in range(rows)])

    pl.semaphore_wait(barrier, n - 1)

    def send_stats(which):
        def send(k, carry):
            pltpu.make_async_remote_copy(
                src_ref=own_stat.at[which],
                dst_ref=in_stat.at[which, k],
                send_sem=stat_send.at[which],
                recv_sem=stat_recv.at[which],
                device_id={"rows": lax.rem(me + k, n)},
                device_id_type=MESH,
            ).start()
            return carry

        lax.fori_loop(1, n, send, 0)
        in_stat[which, 0] = own_stat[which]

    def all_stats(which):
        return pltpu.make_async_remote_copy(
            src_ref=in_stat.at[which, pl.ds(1, n - 1)],
            dst_ref=in_stat.at[which, pl.ds(1, n - 1)],
            send_sem=stat_send.at[which],
            recv_sem=stat_recv.at[which],
            device_id={"rows": lax.rem(me + 1, n)},
            device_id_type=MESH,
        )

    send_stats(0)

    upward = pltpu.make_async_remote_copy(
        src_ref=x.at[pl.ds(2, 2)],
        dst_ref=x.at[pl.ds(2 + rows, 2)],
        send_sem=rim_send.at[0],
        recv_sem=rim_recv.at[0],
        device_id={"rows": lax.rem(me + n - 1, n)},
        device_id_type=MESH,
    )
    downward = pltpu.make_async_remote_copy(
        src_ref=x.at[pl.ds(rows, 2)],
        dst_ref=x.at[pl.ds(0, 2)],
        send_sem=rim_send.at[1],
        recv_sem=rim_recv.at[1],
        device_id={"rows": lax.rem(me + 1, n)},
        device_id_type=MESH,
    )

    @pl.when(me > 0)
    def _():
        upward.start()

    @pl.when(me < n - 1)
    def _():
        downward.start()

    def pair_weights(w, wp):
        zero = jnp.zeros((band, chan), BF16)
        wp[pl.ds(3 * band, band), pl.ds(0, chan)] = zero
        wp[pl.ds(0, band), pl.ds(chan, chan)] = zero
        for tap in range(3):
            at = pl.ds(tap * band, band)
            total = w[0, at].astype(F32) + w[1, at].astype(F32) + w[2, at].astype(F32)
            total = total.astype(BF16)
            wp[at, pl.ds(0, chan)] = total
            wp[pl.ds((tap + 1) * band, band), pl.ds(chan, chan)] = total

    loads[1].wait()
    pair_weights(w1, wp1)
    loads[2].wait()
    pair_weights(w2, wp2)
    for copy in loads[3:]:
        copy.wait()

    @pl.when(me == 0)
    def _():
        for r in range(2):
            x[r] = x[2]

    @pl.when(me == n - 1)
    def _():
        for r in range(2):
            x[2 + rows + r] = x[1 + rows]

    all_stats(0).wait_recv()
    scale, offset = scale_offset(in_stat[0], vec[0], vec[1], count, per_group)

    def activate(row, slot, scale, offset):
        value = silu(row.astype(F32) * scale + offset)
        act[slot, pl.ds(8, width)] = value
        act[slot, pl.ds(7, 1)] = value[0:1]
        act[slot, pl.ds(8 + width, 1)] = value[width - 1 : width]
        base = slot * band
        stack[:, pl.ds(base, chan)] = act[slot, pl.ds(7, width)].astype(BF16)
        stack[:, pl.ds(base + chan, chan)] = value.astype(BF16)
        stack[:, pl.ds(base + 2 * chan, chan)] = act[slot, pl.ds(9, width)].astype(BF16)

    for r in range(2, 2 + rows):
        activate(x[r], r, scale, offset)

    @pl.when(me < n - 1)
    def _():
        upward.wait_recv()

    @pl.when(me > 0)
    def _():
        downward.wait_recv()

    activate(x[1], 1, scale, offset)
    activate(x[2 + rows], 2 + rows, scale, offset)

    def conv_pairs(wp, first, bias):
        out = []
        for pair in range(rows // 2):
            lhs = stack[:, pl.ds((first + 2 * pair) * band, 4 * band)]
            both = jnp.dot(lhs, wp[...], preferred_element_type=F32)
            out.append(both[:, :chan] + bias)
            out.append(both[:, chan:] + bias)
        return out

    hidden = [h.astype(BF16) for h in conv_pairs(wp1, 1, vec[2])]
    for r in range(rows):
        hid[1 + r] = hidden[r]
    own_stat[1] = partial_sums([h.astype(F32) for h in hidden])
    send_stats(1)

    activate(x[0], 0, scale, offset)
    activate(x[3 + rows], 3 + rows, scale, offset)
    for target, first, edge, own in ((0, 0, 0, 1), (1 + rows, 1 + rows, n - 1, rows)):
        lhs = stack[:, pl.ds(first * band, 3 * band)]
        rim = jnp.dot(lhs, wp1[pl.ds(0, 3 * band), pl.ds(0, chan)], preferred_element_type=F32)
        rim = (rim + vec[2]).astype(BF16)
        hid[target] = rim

        @pl.when(me == edge)
        def _():
            hid[target] = hid[own]

    all_stats(1).wait_recv()
    scale, offset = scale_offset(in_stat[1], vec[3], vec[4], count, per_group)
    for r in range(rows + 2):
        activate(hid[r], r, scale, offset)
    branch = conv_pairs(wp2, 0, vec[5])
    for r in range(rows):
        out_ref[0, r] = (x[2 + r].astype(F32) + branch[r]).astype(BF16)

    all_stats(0).wait_send()
    all_stats(1).wait_send()

    @pl.when(me > 0)
    def _():
        upward.wait_send()

    @pl.when(me < n - 1)
    def _():
        downward.wait_send()


def body(latents, gain_one, shift_one, weight_one, bias_one, gain_two, shift_two, weight_two, bias_two):
    n = lax.axis_size("rows")
    frames, rows, width, chan = latents.shape
    per_group = chan // GROUPS
    count = frames * rows * width * per_group * n
    taps = weight_one.shape[0]
    flat = lambda w: w.reshape(taps, 9 * chan, chan)
    line = lambda v: v.reshape(1, chan)
    band = 3 * chan
    anywhere = pl.BlockSpec(memory_space=pltpu.HBM)
    return pl.pallas_call(
        functools.partial(kernel, n, count, per_group),
        out_shape=jax.ShapeDtypeStruct(latents.shape, BF16),
        in_specs=[anywhere] * 9,
        out_specs=pl.BlockSpec(memory_space=pltpu.VMEM),
        scratch_shapes=[
            pltpu.VMEM((rows + 4, width, chan), BF16),
            pltpu.VMEM((taps, 9 * chan, chan), BF16),
            pltpu.VMEM((taps, 9 * chan, chan), BF16),
            pltpu.VMEM((4 * band, 2 * chan), BF16),
            pltpu.VMEM((4 * band, 2 * chan), BF16),
            pltpu.VMEM((6, 1, chan), F32),
            pltpu.VMEM((rows + 4, width + 16, chan), F32),
            pltpu.VMEM((width, (rows + 4) * band), BF16),
            pltpu.VMEM((rows + 2, width, chan), BF16),
            pltpu.VMEM((2, 2, chan), F32),
            pltpu.VMEM((2, n, 2, chan), F32),
            pltpu.SemaphoreType.DMA((9,)),
            pltpu.SemaphoreType.DMA((2,)),
            pltpu.SemaphoreType.DMA((2,)),
            pltpu.SemaphoreType.DMA((2,)),
            pltpu.SemaphoreType.DMA((2,)),
        ],
        compiler_params=pltpu.CompilerParams(
            collective_id=0, has_side_effects=True, vmem_limit_bytes=48 * 1024 * 1024
        ),
    )(
        latents, line(gain_one), line(shift_one), flat(weight_one), line(bias_one),
        line(gain_two), line(shift_two), flat(weight_two), line(bias_two),
    )


def solution(mesh):
    return jax.shard_map(
        body,
        mesh=mesh,
        in_specs=(P("groups", "rows", None, None), P(), P(), P(), P(), P(), P(), P(), P()),
        out_specs=P("groups", "rows", None, None),
        check_vma=False,
    )
```

time: 91.1 us -> 21.6 us (0.24)
  the two profiles are of different devices: /device:TPU:1 before, /device:TPU:0 now
where the time goes in v1:
time: 21.6 us; the launch traced here: 21.3 us
  Pallas kernels  16.6 us (77%)
  local copies, waits for them, and re-layouts  4.71 us (22%)
    pallas_call x1, Pallas kernels, body(): pl.pallas_call(functools.partial(kernel, n, count, per_group), out_shape=...  16.6 us
    unnamed x19, local copies, waits for them, and re-layouts  4.71 us

profile of v1, /device:TPU:0, one launch (start us, length us, event | category | flops | bytes accessed | tf_op | source)
XLA Modules:
  0.0 21.3 jit_solution(10735581107112009900)
XLA Ops:
  0.0 0.0 copy-start.6
  0.0 0.0 copy-start.7
  0.0 0.0 copy-start.8
  0.0 0.0 copy-start.3
  0.0 0.0 copy-start.4
  0.0 0.0 copy-start.5
  0.0 0.6 %copy-done.6 = f32[128]{0:T(128)S(1)} copy-done((f32[128]{0:T(128)S(1)}, f32[128]{0:T(128)}, u32[]{:S(2)}) %copy-start.6) | copy-done | bytes 536
  0.7 0.0 copy-done.7
  0.7 0.0 copy-done.8
  0.7 0.0 copy-done.3
  0.7 0.0 copy-done.4
  0.7 0.0 copy-done.5
  0.7 0.0 copy-start
  0.7 1.2 %copy-done = bf16[3,3,3,128,128]{4,3,2,1,0:T(8,128)(2,1)S(1)} copy-done((bf16[3,3,3,128,128]{4,3,2,1,0:T(8,128)(2,1)S(1)}, bf16[3,3,3,128,128]{4,3,2,1,0:T(8,128)(2,1)}, u32[]{:S(2)}) %copy-start) | copy-done | bytes 884760
  1.9 0.0 copy-start.1
  1.9 1.2 %copy-done.1 = bf16[3,3,3,128,128]{4,3,2,1,0:T(8,128)(2,1)S(1)} copy-done((bf16[3,3,3,128,128]{4,3,2,1,0:T(8,128)(2,1)S(1)}, bf16[3,3,3,128,128]{4,3,2,1,0:T(8,128)(2,1)}, u32[]{:S(2)}) %copy-start.1) | copy-done | bytes 884760
  3.1 0.0 copy-start.2
  3.1 0.9 %copy-done.2 = bf16[1,4,256,128]{3,2,1,0:T(8,128)(2,1)S(1)} copy-done((bf16[1,4,256,128]{3,2,1,0:T(8,128)(2,1)S(1)}, bf16[1,4,256,128]{3,2,1,0:T(8,128)(2,1)}, u32[]{:S(2)}) %copy-start.2) | copy-done | bytes 262168
  4.0 16.6 %shard_map.91 = bf16[1,4,256,128]{3,2,1,0:T(8,128)(2,1)S(1)} custom-call(bf16[1,4,256,128]{3,2,1,0:T(8,128)(2,1)S(1)} %copy-done.2, f32[1,128]{1,0:T(1,128)S(1)} %bitcast.10, f32[1,128]{1,0:T(1,128)S(1)} %bitcast.11, bf16[3,1152,128]{2,1,0:T(8,128)(2,1)S(1)} %bitcast.8, f32[1,128]{1,0:T(1,128)S(1)} %bitcast.12, f32[1,128]{1,0:T(1,128)S(1)} %bitcast.13, ...), custom_call_target="tpu_custom_call" | custom-call | tf_op jit(solution)/shard_map/pallas_call | solution.py:256
  20.6 0.7 %copy.11 = bf16[1,4,256,128]{3,2,1,0:T(8,128)(2,1)} copy(bf16[1,4,256,128]{3,2,1,0:T(8,128)(2,1)S(1)} %shard_map.91) | data formatting | bytes 524288
Async XLA Ops:
  0.0 0.7 %copy-start.6 = (f32[128]{0:T(128)S(1)}, f32[128]{0:T(128)}, u32[]{:S(2)}) copy-start(f32[128]{0:T(128)} %param.14) | copy-start | bytes 1540
  0.0 0.7 %copy-start.7 = (f32[128]{0:T(128)S(1)}, f32[128]{0:T(128)}, u32[]{:S(2)}) copy-start(f32[128]{0:T(128)} %param.15) | copy-start | bytes 1540
  0.0 0.7 %copy-start.8 = (f32[128]{0:T(128)S(1)}, f32[128]{0:T(128)}, u32[]{:S(2)}) copy-start(f32[128]{0:T(128)} %param.17) | copy-start | bytes 1540
  0.0 0.7 %copy-start.3 = (f32[128]{0:T(128)S(1)}, f32[128]{0:T(128)}, u32[]{:S(2)}) copy-start(f32[128]{0:T(128)} %param.10) | copy-start | bytes 1540
  0.0 0.7 %copy-start.4 = (f32[128]{0:T(128)S(1)}, f32[128]{0:T(128)}, u32[]{:S(2)}) copy-start(f32[128]{0:T(128)} %param.11) | copy-start | bytes 1540
  0.0 0.7 %copy-start.5 = (f32[128]{0:T(128)S(1)}, f32[128]{0:T(128)}, u32[]{:S(2)}) copy-start(f32[128]{0:T(128)} %param.13) | copy-start | bytes 1540
  0.7 1.2 %copy-start = (bf16[3,3,3,128,128]{4,3,2,1,0:T(8,128)(2,1)S(1)}, bf16[3,3,3,128,128]{4,3,2,1,0:T(8,128)(2,1)}, u32[]{:S(2)}) copy-start(bf16[3,3,3,128,128]{4,3,2,1,0:T(8,128)(2,1)} %param.12) | copy-start | bytes 2654212
  1.9 1.2 %copy-start.1 = (bf16[3,3,3,128,128]{4,3,2,1,0:T(8,128)(2,1)S(1)}, bf16[3,3,3,128,128]{4,3,2,1,0:T(8,128)(2,1)}, u32[]{:S(2)}) copy-start(bf16[3,3,3,128,128]{4,3,2,1,0:T(8,128)(2,1)} %param.16) | copy-start | bytes 2654212
  3.1 0.9 %copy-start.2 = (bf16[1,4,256,128]{3,2,1,0:T(8,128)(2,1)S(1)}, bf16[1,4,256,128]{3,2,1,0:T(8,128)(2,1)}, u32[]{:S(2)}) copy-start(bf16[1,4,256,128]{3,2,1,0:T(8,128)(2,1)} %x_hbm.1) | copy-start | bytes 786436

commit v2 on v1

--- a/solution.py
+++ b/solution.py
@@ -11,6 +11,7 @@
 MESH = pl.DeviceIdType.MESH
 F32 = jnp.float32
 BF16 = jnp.bfloat16
+VMEM_BYTES = (64 * 1024 - 10720) * 1024
 
 
 def partial_sums(rows):
@@ -42,12 +43,12 @@
     totals = group_total(jnp.sum(slots, axis=0), per_group)
     mean = totals[0:1] / count
     var = totals[1:2] / count - mean * mean
-    scale = gain / jnp.sqrt(var + 1e-06)
-    return scale, shift - mean * scale
-
-
-def silu(values):
-    return values / (1.0 + jnp.exp(-values))
+    scale = (0.5 * gain) / jnp.sqrt(var + 1e-06)
+    return scale, 0.5 * shift - mean * scale
+
+
+def silu_of_double(half):
+    return half + half * jnp.tanh(half)
 
 
 def kernel(
@@ -66,6 +67,20 @@
     band = 3 * chan
     vec_hbm = (g1_hbm, s1_hbm, b1_hbm, g2_hbm, s2_hbm, b2_hbm)
 
+    low = jnp.where(me < n // 2, 1, 0)
+
+    def other(k):
+        place = low * (n - 1 - k) + (1 - low) * k
+        return place + jnp.where(low == 1, jnp.where(place <= me, -1, 0), jnp.where(place >= me, 1, 0))
+
+    barrier = pltpu.get_barrier_semaphore()
+
+    def greet(k, carry):
+        pl.semaphore_signal(barrier, inc=1, device_id={"rows": other(k)}, device_id_type=MESH)
+        return carry
+
+    lax.fori_loop(0, n - 1, greet, 0)
+
     loads = [pltpu.make_async_copy(x_hbm.at[0], x.at[pl.ds(2, rows)], load_sem.at[0])]
     loads.append(pltpu.make_async_copy(w1_hbm, w1, load_sem.at[1]))
     loads.append(pltpu.make_async_copy(w2_hbm, w2, load_sem.at[2]))
@@ -74,35 +89,57 @@
     for copy in loads:
         copy.start()
 
-    barrier = pltpu.get_barrier_semaphore()
-
-    def greet(k, carry):
-        pl.semaphore_signal(
-            barrier, inc=1, device_id={"rows": lax.rem(me + k, n)}, device_id_type=MESH
+    pl.semaphore_wait(barrier, n - 1)
+
+    up_id = {"rows": lax.rem(me + n - 1, n)}
+    down_id = {"rows": lax.rem(me + 1, n)}
+
+    def rim(source, target, device, sem):
+        return pltpu.make_async_remote_copy(
+            src_ref=x_hbm.at[0, pl.ds(source, 1)],
+            dst_ref=x.at[pl.ds(target, 1)],
+            send_sem=rim_send.at[sem],
+            recv_sem=rim_recv.at[sem],
+            device_id=device,
+            device_id_type=MESH,
         )
-        return carry
-
-    lax.fori_loop(1, n, greet, 0)
-
-    loads[0].wait()
-    own_stat[0] = partial_sums([x[2 + r].astype(F32) for r in range(rows)])
-
-    pl.semaphore_wait(barrier, n - 1)
+
+    upward = [rim(i, 2 + rows + i, up_id, i) for i in range(2)]
+    downward = [rim(rows - 1 - i, 1 - i, down_id, 2 + i) for i in range(2)]
+    for i in range(2):
+
+        @pl.when(me > 0)
+        def _():
+            upward[i].start()
+
+        @pl.when(me < n - 1)
+        def _():
+            downward[i].start()
+
+    def rims_arrive(i):
+        @pl.when(me < n - 1)
+        def _():
+            upward[i].wait_recv()
+
+        @pl.when(me > 0)
+        def _():
+            downward[i].wait_recv()
 
     def send_stats(which):
         def send(k, carry):
+            target = other(k)
             pltpu.make_async_remote_copy(
                 src_ref=own_stat.at[which],
-                dst_ref=in_stat.at[which, k],
+                dst_ref=in_stat.at[which, me],
                 send_sem=stat_send.at[which],
                 recv_sem=stat_recv.at[which],
-                device_id={"rows": lax.rem(me + k, n)},
+                device_id={"rows": target},
                 device_id_type=MESH,
             ).start()
             return carry
 
-        lax.fori_loop(1, n, send, 0)
-        in_stat[which, 0] = own_stat[which]
+        lax.fori_loop(0, n - 1, send, 0)
+        in_stat[which, me] = own_stat[which]
 
     def all_stats(which):
         return pltpu.make_async_remote_copy(
@@ -114,32 +151,9 @@
             device_id_type=MESH,
         )
 
+    loads[0].wait()
+    own_stat[0] = partial_sums([x[2 + r].astype(F32) for r in range(rows)])
     send_stats(0)
-
-    upward = pltpu.make_async_remote_copy(
-        src_ref=x.at[pl.ds(2, 2)],
-        dst_ref=x.at[pl.ds(2 + rows, 2)],
-        send_sem=rim_send.at[0],
-        recv_sem=rim_recv.at[0],
-        device_id={"rows": lax.rem(me + n - 1, n)},
-        device_id_type=MESH,
-    )
-    downward = pltpu.make_async_remote_copy(
-        src_ref=x.at[pl.ds(rows, 2)],
-        dst_ref=x.at[pl.ds(0, 2)],
-        send_sem=rim_send.at[1],
-        recv_sem=rim_recv.at[1],
-        device_id={"rows": lax.rem(me + 1, n)},
-        device_id_type=MESH,
-    )
-
-    @pl.when(me > 0)
-    def _():
-        upward.start()
-
-    @pl.when(me < n - 1)
-    def _():
-        downward.start()
 
     def pair_weights(w, wp):
         zero = jnp.zeros((band, chan), BF16)
@@ -173,7 +187,7 @@
     scale, offset = scale_offset(in_stat[0], vec[0], vec[1], count, per_group)
 
     def activate(row, slot, scale, offset):
-        value = silu(row.astype(F32) * scale + offset)
+        value = silu_of_double(row.astype(F32) * scale + offset)
         act[slot, pl.ds(8, width)] = value
         act[slot, pl.ds(7, 1)] = value[0:1]
         act[slot, pl.ds(8 + width, 1)] = value[width - 1 : width]
@@ -185,14 +199,7 @@
     for r in range(2, 2 + rows):
         activate(x[r], r, scale, offset)
 
-    @pl.when(me < n - 1)
-    def _():
-        upward.wait_recv()
-
-    @pl.when(me > 0)
-    def _():
-        downward.wait_recv()
-
+    rims_arrive(0)
     activate(x[1], 1, scale, offset)
     activate(x[2 + rows], 2 + rows, scale, offset)
 
@@ -211,6 +218,7 @@
     own_stat[1] = partial_sums([h.astype(F32) for h in hidden])
     send_stats(1)
 
+    rims_arrive(1)
     activate(x[0], 0, scale, offset)
     activate(x[3 + rows], 3 + rows, scale, offset)
     for target, first, edge, own in ((0, 0, 0, 1), (1 + rows, 1 + rows, n - 1, rows)):
@@ -234,13 +242,15 @@
     all_stats(0).wait_send()
     all_stats(1).wait_send()
 
-    @pl.when(me > 0)
-    def _():
-        upward.wait_send()
-
-    @pl.when(me < n - 1)
-    def _():
-        downward.wait_send()
+    for i in range(2):
+
+        @pl.when(me > 0)
+        def _():
+            upward[i].wait_send()
+
+        @pl.when(me < n - 1)
+        def _():
+            downward[i].wait_send()
 
 
 def body(latents, gain_one, shift_one, weight_one, bias_one, gain_two, shift_two, weight_two, bias_two):
@@ -252,7 +262,7 @@
     flat = lambda w: w.reshape(taps, 9 * chan, chan)
     line = lambda v: v.reshape(1, chan)
     band = 3 * chan
-    anywhere = pl.BlockSpec(memory_space=pltpu.HBM)
+    anywhere = pl.BlockSpec(memory_space=pl.ANY)
     return pl.pallas_call(
         functools.partial(kernel, n, count, per_group),
         out_shape=jax.ShapeDtypeStruct(latents.shape, BF16),
@@ -273,11 +283,11 @@
             pltpu.SemaphoreType.DMA((9,)),
             pltpu.SemaphoreType.DMA((2,)),
             pltpu.SemaphoreType.DMA((2,)),
-            pltpu.SemaphoreType.DMA((2,)),
-            pltpu.SemaphoreType.DMA((2,)),
+            pltpu.SemaphoreType.DMA((4,)),
+            pltpu.SemaphoreType.DMA((4,)),
         ],
         compiler_params=pltpu.CompilerParams(
-            collective_id=0, has_side_effects=True, vmem_limit_bytes=48 * 1024 * 1024
+            collective_id=0, has_side_effects=True, vmem_limit_bytes=VMEM_BYTES
         ),
     )(
         latents, line(gain_one), line(shift_one), flat(weight_one), line(bias_one),

time: 21.6 us -> 18 us (0.83)
  local copies, waits for them, and re-layouts: 4.71 us -> 1.42 us
    unnamed x19 -> x13, local copies, waits for them, and re-layouts: 4.71 us -> 1.42 us
where the time goes in v2:
time: 18 us; the launch traced here: 17.8 us
  Pallas kernels  16.4 us (91%)
  local copies, waits for them, and re-layouts  1.42 us (8%)
    pallas_call x1, Pallas kernels, body(): pl.pallas_call(functools.partial(kernel, n, count, per_group), out_shape=...  16.4 us
    unnamed x13, local copies, waits for them, and re-layouts  1.42 us

profile of v2, /device:TPU:0, one launch (start us, length us, event | category | flops | bytes accessed | tf_op | source)
XLA Modules:
  0.0 17.8 jit_solution(8480130038928759555)
XLA Ops:
  0.0 0.0 copy-start.3
  0.0 0.0 copy-start.4
  0.0 0.0 copy-start.5
  0.0 0.0 copy-start
  0.0 0.0 copy-start.1
  0.0 0.0 copy-start.2
  0.0 0.6 %copy-done.3 = f32[128]{0:T(128)S(1)} copy-done((f32[128]{0:T(128)S(1)}, f32[128]{0:T(128)}, u32[]{:S(2)}) %copy-start.3) | copy-done | bytes 536
  0.7 0.0 copy-done.4
  0.7 0.0 copy-done.5
  0.7 0.0 copy-done
  0.7 0.0 copy-done.1
  0.7 0.0 copy-done.2
  0.7 16.4 %shard_map.91 = bf16[1,4,256,128]{3,2,1,0:T(8,128)(2,1)S(1)} custom-call(bf16[1,4,256,128]{3,2,1,0:T(8,128)(2,1)} %x_hbm.1, f32[1,128]{1,0:T(1,128)S(1)} %bitcast.8, f32[1,128]{1,0:T(1,128)S(1)} %bitcast.9, bf16[3,1152,128]{2,1,0:T(8,128)(2,1)} %bitcast.14, f32[1,128]{1,0:T(1,128)S(1)} %bitcast.10, f32[1,128]{1,0:T(1,128)S(1)} %bitcast.11, ...), custom_call_target="tpu_custom_call" | custom-call | tf_op jit(solution)/shard_map/pallas_call | solution.py:266
  17.1 0.7 %copy.11 = bf16[1,4,256,128]{3,2,1,0:T(8,128)(2,1)} copy(bf16[1,4,256,128]{3,2,1,0:T(8,128)(2,1)S(1)} %shard_map.91) | data formatting | bytes 524288
Async XLA Ops:
  0.0 0.7 %copy-start.3 = (f32[128]{0:T(128)S(1)}, f32[128]{0:T(128)}, u32[]{:S(2)}) copy-start(f32[128]{0:T(128)} %param.14) | copy-start | bytes 1540
  0.0 0.7 %copy-start.4 = (f32[128]{0:T(128)S(1)}, f32[128]{0:T(128)}, u32[]{:S(2)}) copy-start(f32[128]{0:T(128)} %param.15) | copy-start | bytes 1540
  0.0 0.7 %copy-start.5 = (f32[128]{0:T(128)S(1)}, f32[128]{0:T(128)}, u32[]{:S(2)}) copy-start(f32[128]{0:T(128)} %param.17) | copy-start | bytes 1540
  0.0 0.7 %copy-start = (f32[128]{0:T(128)S(1)}, f32[128]{0:T(128)}, u32[]{:S(2)}) copy-start(f32[128]{0:T(128)} %param.10) | copy-start | bytes 1540
  0.0 0.7 %copy-start.1 = (f32[128]{0:T(128)S(1)}, f32[128]{0:T(128)}, u32[]{:S(2)}) copy-start(f32[128]{0:T(128)} %param.11) | copy-start | bytes 1540
  0.0 0.7 %copy-start.2 = (f32[128]{0:T(128)S(1)}, f32[128]{0:T(128)}, u32[]{:S(2)}) copy-start(f32[128]{0:T(128)} %param.13) | copy-start | bytes 1540

commit v3 on v2

--- a/solution.py
+++ b/solution.py
@@ -106,8 +106,7 @@
 
     upward = [rim(i, 2 + rows + i, up_id, i) for i in range(2)]
     downward = [rim(rows - 1 - i, 1 - i, down_id, 2 + i) for i in range(2)]
-    for i in range(2):
-
+    def send_rims(i):
         @pl.when(me > 0)
         def _():
             upward[i].start()
@@ -154,6 +153,8 @@
     loads[0].wait()
     own_stat[0] = partial_sums([x[2 + r].astype(F32) for r in range(rows)])
     send_stats(0)
+    send_rims(0)
+    send_rims(1)
 
     def pair_weights(w, wp):
         zero = jnp.zeros((band, chan), BF16)
@@ -168,8 +169,6 @@
 
     loads[1].wait()
     pair_weights(w1, wp1)
-    loads[2].wait()
-    pair_weights(w2, wp2)
     for copy in loads[3:]:
         copy.wait()
 
@@ -218,6 +217,8 @@
     own_stat[1] = partial_sums([h.astype(F32) for h in hidden])
     send_stats(1)
 
+    loads[2].wait()
+    pair_weights(w2, wp2)
     rims_arrive(1)
     activate(x[0], 0, scale, offset)
     activate(x[3 + rows], 3 + rows, scale, offset)

time: 18 us -> 17.7 us (0.983)
  Pallas kernels: 16.4 us -> 16.1 us
    pallas_call x1, Pallas kernels: 16.4 us -> 16.1 us  [body(): pl.pallas_call(functools.partial(kernel, n, count, per_group), out_shape=...]
where the time goes in v3:
time: 17.7 us; the launch traced here: 17.5 us
  Pallas kernels  16.1 us (91%)
  local copies, waits for them, and re-layouts  1.42 us (8%)
    pallas_call x1, Pallas kernels, body(): pl.pallas_call(functools.partial(kernel, n, count, per_group), out_shape=...  16.1 us
    unnamed x13, local copies, waits for them, and re-layouts  1.42 us

profile of v3, /device:TPU:0, one launch (start us, length us, event | category | flops | bytes accessed | tf_op | source)
XLA Modules:
  0.0 17.5 jit_solution(7659174601709140814)
XLA Ops:
  0.0 0.0 copy-start.3
  0.0 0.0 copy-start.4
  0.0 0.0 copy-start.5
  0.0 0.0 copy-start
  0.0 0.0 copy-start.1
  0.0 0.0 copy-start.2
  0.0 0.6 %copy-done.3 = f32[128]{0:T(128)S(1)} copy-done((f32[128]{0:T(128)S(1)}, f32[128]{0:T(128)}, u32[]{:S(2)}) %copy-start.3) | copy-done | bytes 536
  0.7 0.0 copy-done.4
  0.7 0.0 copy-done.5
  0.7 0.0 copy-done
  0.7 0.0 copy-done.1
  0.7 0.0 copy-done.2
  0.7 16.1 %shard_map.91 = bf16[1,4,256,128]{3,2,1,0:T(8,128)(2,1)S(1)} custom-call(bf16[1,4,256,128]{3,2,1,0:T(8,128)(2,1)} %x_hbm.1, f32[1,128]{1,0:T(1,128)S(1)} %bitcast.8, f32[1,128]{1,0:T(1,128)S(1)} %bitcast.9, bf16[3,1152,128]{2,1,0:T(8,128)(2,1)} %bitcast.14, f32[1,128]{1,0:T(1,128)S(1)} %bitcast.10, f32[1,128]{1,0:T(1,128)S(1)} %bitcast.11, ...), custom_call_target="tpu_custom_call" | custom-call | tf_op jit(solution)/shard_map/pallas_call | solution.py:267
  16.8 0.7 %copy.11 = bf16[1,4,256,128]{3,2,1,0:T(8,128)(2,1)} copy(bf16[1,4,256,128]{3,2,1,0:T(8,128)(2,1)S(1)} %shard_map.91) | data formatting | bytes 524288
Async XLA Ops:
  0.0 0.7 %copy-start.3 = (f32[128]{0:T(128)S(1)}, f32[128]{0:T(128)}, u32[]{:S(2)}) copy-start(f32[128]{0:T(128)} %param.14) | copy-start | bytes 1540
  0.0 0.7 %copy-start.4 = (f32[128]{0:T(128)S(1)}, f32[128]{0:T(128)}, u32[]{:S(2)}) copy-start(f32[128]{0:T(128)} %param.15) | copy-start | bytes 1540
  0.0 0.7 %copy-start.5 = (f32[128]{0:T(128)S(1)}, f32[128]{0:T(128)}, u32[]{:S(2)}) copy-start(f32[128]{0:T(128)} %param.17) | copy-start | bytes 1540
  0.0 0.7 %copy-start = (f32[128]{0:T(128)S(1)}, f32[128]{0:T(128)}, u32[]{:S(2)}) copy-start(f32[128]{0:T(128)} %param.10) | copy-start | bytes 1540
  0.0 0.7 %copy-start.1 = (f32[128]{0:T(128)S(1)}, f32[128]{0:T(128)}, u32[]{:S(2)}) copy-start(f32[128]{0:T(128)} %param.11) | copy-start | bytes 1540
  0.0 0.7 %copy-start.2 = (f32[128]{0:T(128)S(1)}, f32[128]{0:T(128)}, u32[]{:S(2)}) copy-start(f32[128]{0:T(128)} %param.13) | copy-start | bytes 1540
